TPU v7x, 256 devices: a whole 4x4x8 slice. The times are simulated.
256 devices in a mesh: pipe: 8 (over x_lo, y), expert: 16 (over z, x_hi), dp: 2 (over core).
Axes of the slice: x: 4 (x_hi: 2, x_lo: 2; x = x_hi * 2 + x_lo), y: 4, z: 8, core: 2. Of those that a mesh axis runs over, the one named last changes fastest.
Arguments:
- states: bfloat16 [16, 1024, 3584], P(('pipe', 'dp'), 'expert'), may hold values from -6 to 6
- norm_gain: float32 [16, 3584], P(('pipe', 'dp')), may hold values from 0.4 to 1.6
- w_in: bfloat16 [16, 16, 3584, 1024], P(('pipe', 'dp'), 'expert'), may hold values from -0.09375 to 0.09375
- w_out: bfloat16 [16, 16, 512, 3584], P(('pipe', 'dp'), 'expert'), may hold values from -0.1875 to 0.1875
- routes: int32 [16, 2, 1024, 2], P(('pipe', 'dp'), None, 'expert'), may hold values from 0 to 7, all different within a row; in each aligned block of 64 rows (0 to 63, 64 to 127, ..., all dimensions but the last counted through in order) at most 20 rows name the same one
- route_weights: float32 [16, 2, 1024, 2], P(('pipe', 'dp'), None, 'expert'), may hold values from 0.2 to 1
Outputs:
- section_outputs: bfloat16 [16, 1024, 3584], P(('pipe', 'dp'), 'expert')
Inputs may be any that keep to these rules, and one draw needn't show every extreme that they name: `routes`: each row names 2 different experts. In each aligned block of 64 rows (the tokens of one index of expert at one section and step) no expert is named by more than 20 rows.
All inputs are finite; a program needn't handle non-finite values.
Results may differ from a plain program's by a relative error of at most 0.0075.
Values may be sent and summed in bfloat16 or wider, within the bound.
A program may use at most 64 MiB of HBM per device.

v0:
```python
import jax
import jax.numpy as jnp
from jax import lax
from jax.sharding import PartitionSpec as P

STEPS = 2


EPS = 1e-06


def shifted(block, axis, distance):
    devices = range(lax.axis_size(axis))
    route = [(i - distance, i) for i in devices if i - distance in devices]
    return lax.ppermute(block, axis, route)


def slot_index(route_block, experts):
    onehot = (route_block[:, :, None] == jnp.arange(experts, dtype=jnp.int32)).astype(jnp.int32)
    per_token = jnp.sum(onehot, axis=1)
    earlier = jnp.cumsum(per_token, axis=0) - per_token
    return jnp.sum(onehot * earlier[:, None, :], axis=2)


def expert_partial(token_rows, weight_in, weight_out):
    row_shape = token_rows.shape
    flat_rows = token_rows.reshape(-1, row_shape[-1])
    both = jnp.dot(flat_rows, weight_in, preferred_element_type=jnp.float32)
    hidden_width = weight_out.shape[0]
    hidden = (jax.nn.silu(both[:, :hidden_width]) * both[:, hidden_width:]).astype(jnp.bfloat16)
    partial_value = jnp.dot(hidden, weight_out, preferred_element_type=jnp.float32).astype(
        jnp.bfloat16
    )
    return partial_value.reshape(row_shape)


def run_section(current, gain, weight_in, weight_out, route_block, route_weight):
    n_expert = lax.axis_size("expert")
    experts = n_expert // 2
    tokens, width = current.shape
    routed = route_block.shape[1]
    capacity = min(tokens, 5 * tokens * routed // (4 * experts))
    current_f = current.astype(jnp.float32)
    normed = (
        current_f * lax.rsqrt(jnp.mean(current_f * current_f, axis=-1, keepdims=True) + EPS) * gain
    ).astype(jnp.bfloat16)
    flat = route_block * capacity + slot_index(route_block, experts)
    copies = jnp.broadcast_to(normed[:, None, :], (tokens, routed, width)).reshape(
        tokens * routed, width
    )
    buffer = jnp.zeros((experts * capacity, width), jnp.bfloat16).at[flat.reshape(-1)].set(copies)
    outgoing = jnp.broadcast_to(
        buffer.reshape(experts, 1, capacity, width), (experts, 2, capacity, width)
    ).reshape(n_expert, capacity, width)
    partial_value = expert_partial(
        lax.all_to_all(outgoing, "expert", split_axis=0, concat_axis=0, tiled=True),
        weight_in,
        weight_out,
    )
    returned = lax.all_to_all(partial_value, "expert", split_axis=0, concat_axis=0, tiled=True)
    expert_out = (
        jnp.sum(returned.reshape(experts, 2, capacity, width).astype(jnp.float32), axis=1)
        .astype(jnp.bfloat16)
        .reshape(experts * capacity, width)
    )
    picked = jnp.take(expert_out, flat.reshape(-1), axis=0).reshape(tokens, routed, width)
    mixed = current_f + jnp.sum(route_weight[:, :, None] * picked.astype(jnp.float32), axis=1)
    return mixed.astype(jnp.bfloat16)


def body(states, norm_gain, w_in, w_out, routes, route_weights):
    pipe_rank = lax.axis_index("pipe")
    copy_index = lax.axis_index("dp")
    last_rank = lax.axis_size("pipe") - 1
    current = states[0]
    produced = current
    for step_index in range(STEPS):
        produced = run_section(
            current,
            norm_gain[0],
            w_in[0, 0],
            w_out[0, 0],
            routes[0, step_index],
            route_weights[0, step_index],
        )
        if step_index + 1 < STEPS:
            from_below = shifted(produced, "pipe", 1)
            from_above = shifted(produced, "pipe", -1)
            from_twin = shifted(produced, "dp", 1)
            current = jnp.where(
                copy_index == 0,
                from_below,
                jnp.where(pipe_rank == last_rank, from_twin, from_above),
            )
    return produced[None]


def solution(mesh):
    in_specs = (
        P(("pipe", "dp"), "expert", None),
        P(("pipe", "dp"), None),
        P(("pipe", "dp"), "expert", None, None),
        P(("pipe", "dp"), "expert", None, None),
        P(("pipe", "dp"), None, "expert", None),
        P(("pipe", "dp"), None, "expert", None),
    )
    out_specs = P(("pipe", "dp"), "expert", None)
    return jax.shard_map(body, mesh=mesh, in_specs=in_specs, out_specs=out_specs, check_vma=False)
```

profile of v0, /device:TPU:2, one launch (start us, length us, event | category | flops | bytes accessed | tf_op | source)
XLA Modules:
  0.0 366.7 jit_solution(11502542406470022535)
XLA Ops:
  0.0 1.2 fusion.10
  1.2 0.7 slice_bitcast_fusion.3
  3.0 0.8 reduce.2
  3.7 1.2 fusion.12
  4.9 0.5 broadcast_in_dim.23
  5.4 0.3 reshape.232
  5.8 2.2 scatter_custom_fusion
  8.0 0.3 broadcast_in_dim.24
  8.3 0.2 broadcast_in_dim.25
  8.5 77.2 %all_to_all.20 = bf16[16,20,3584]{2,1,0:T(8,128)(2,1)S(1)} all-to-all(bf16[16,20,3584]{2,1,0:T(8,128)(2,1)S(1)} %bitcast.47), channel_id=1, replica_groups=mesh['pipe'=8,'expert'=16,'dp'=2] {'expert'}, dimensions={0} | all-to-all | bytes 4587520 | tf_op jit(solution)/shard_map/all_to_all | solution.py:56
  85.7 2.1 reshape.199
  87.8 6.4 %fusion.2 = f32[320,1024]{1,0:T(8,128)S(1)} fusion(bf16[320,3584]{1,0:T(8,128)(2,1)} %reshape.199, bf16[1,1,3584,1024]{3,2,1,0:T(8,128)(2,1)} %param.10), kind=kOutput, calls=%fused_computation.6 | convolution fusion | flops 2348810240 | bytes 10944512 | tf_op jit(solution)/shard_map/dot_general | solution.py:28
  94.3 1.4 convolution_convert_fusion.1
  95.7 2.2 reshape.200
  97.9 4.0 %all-to-all-start.1 = ((bf16[16,20,3584]{2,1,0:T(8,128)(2,1)}), bf16[16,20,3584]{2,1,0:T(8,128)(2,1)S(1)}, u32[]{:S(2)}, u32[]{:S(2)}) async-start(bf16[16,20,3584]{2,1,0:T(8,128)(2,1)} %reshape.200), calls=%async_computation.1 | async-start | bytes 5505024 | tf_op jit(solution)/shard_map/all_to_all | solution.py:60
  102.4 63.8 %all-to-all-done.1 = bf16[16,20,3584]{2,1,0:T(8,128)(2,1)S(1)} async-done(((bf16[16,20,3584]{2,1,0:T(8,128)(2,1)}), bf16[16,20,3584]{2,1,0:T(8,128)(2,1)S(1)}, u32[]{:S(2)}, u32[]{:S(2)}) %all-to-all-start.1) | async-done | bytes 2293792 | tf_op jit(solution)/shard_map/all_to_all | solution.py:60
  166.2 1.7 bitcast_reduce_fusion.1
  167.9 1.4 reshape.202
  169.4 1.1 gather_fusion
  170.5 0.2 select_convert_fusion.1
  170.7 2.3 reshape.210
  173.0 4.1 %multiply_reduce_fusion.1 = f32[64,3584]{1,0:T(8,128)S(1)} fusion(f32[64,2,3584]{2,1,0:T(2,128)} %reshape.210, f32[64,2]{1,0:T(8,128)S(1)} %copy.23), kind=kLoop, calls=%fused_computation.15 | loop fusion | flops 688128 | bytes 2753024 | tf_op jit(solution)/shard_map/reduce_sum | solution.py:67
  177.2 5.8 %collective-permute-start.2 = (bf16[64,3584]{1,0:T(8,128)(2,1)S(1)}, bf16[64,3584]{1,0:T(8,128)(2,1)S(1)}, u32[]{:S(2)}, u32[]{:S(2)}) collective-permute-start(bf16[64,3584]{1,0:T(8,128)(2,1)S(1)} %fusion.13), channel_id=1, source_target_pairs={{32,0},{64,32},{96,64},{128,96},{160,128},{192,160},{224,192},{33,... | collective-permute-start | bytes 1376264 | tf_op jit(solution)/shard_map/ppermute | solution.py:15
  183.0 1.3 collective-permute-start.1
  184.4 1.9 collective-permute-start
  186.8 4.1 %collective-permute-done.2 = bf16[64,3584]{1,0:T(8,128)(2,1)S(1)} collective-permute-done((bf16[64,3584]{1,0:T(8,128)(2,1)S(1)}, bf16[64,3584]{1,0:T(8,128)(2,1)S(1)}, u32[]{:S(2)}, u32[]{:S(2)}) %collective-permute-start.2) | collective-permute-done | bytes 458784 | tf_op jit(solution)/shard_map/ppermute | solution.py:15
  190.9 7.5 %collective-permute-done = bf16[64,3584]{1,0:T(8,128)(2,1)S(1)} collective-permute-done((bf16[64,3584]{1,0:T(8,128)(2,1)S(1)}, bf16[64,3584]{1,0:T(8,128)(2,1)S(1)}, u32[]{:S(2)}, u32[]{:S(2)}) %collective-permute-start) | collective-permute-done | bytes 458784 | tf_op jit(solution)/shard_map/ppermute | solution.py:15
  198.5 0.3 fusion.6
  198.8 0.2 fusion.8
  199.0 0.5 broadcast_in_dim.26
  199.5 1.3 reshape.240
  200.7 2.8 scatter_custom_fusion.1
  203.6 0.3 broadcast_in_dim.27
  203.9 0.2 broadcast_in_dim.28
  204.1 71.5 %all_to_all.21 = bf16[16,20,3584]{2,1,0:T(8,128)(2,1)S(1)} all-to-all(bf16[16,20,3584]{2,1,0:T(8,128)(2,1)S(1)} %bitcast.48), channel_id=1, replica_groups=mesh['pipe'=8,'expert'=16,'dp'=2] {'expert'}, dimensions={0} | all-to-all | bytes 4587520 | tf_op jit(solution)/shard_map/all_to_all | solution.py:56
  275.6 2.1 reshape.205
  277.7 6.4 %fusion = f32[320,1024]{1,0:T(8,128)S(1)} fusion(bf16[320,3584]{1,0:T(8,128)(2,1)} %reshape.205, bf16[1,1,3584,1024]{3,2,1,0:T(8,128)(2,1)} %param.10), kind=kOutput, calls=%fused_computation.4 | convolution fusion | flops 2348810240 | bytes 10944512 | tf_op jit(solution)/shard_map/dot_general | solution.py:28
  284.1 1.4 convolution_convert_fusion
  285.5 2.2 reshape.206
  287.8 3.7 %all-to-all-start.3 = ((bf16[16,20,3584]{2,1,0:T(8,128)(2,1)}), bf16[16,20,3584]{2,1,0:T(8,128)(2,1)S(1)}, u32[]{:S(2)}, u32[]{:S(2)}) async-start(bf16[16,20,3584]{2,1,0:T(8,128)(2,1)} %reshape.206), calls=%async_computation.3 | async-start | bytes 5505024 | tf_op jit(solution)/shard_map/all_to_all | solution.py:60
  291.9 63.0 %all-to-all-done.3 = bf16[16,20,3584]{2,1,0:T(8,128)(2,1)S(1)} async-done(((bf16[16,20,3584]{2,1,0:T(8,128)(2,1)}), bf16[16,20,3584]{2,1,0:T(8,128)(2,1)S(1)}, u32[]{:S(2)}, u32[]{:S(2)}) %all-to-all-start.3) | async-done | bytes 2293792 | tf_op jit(solution)/shard_map/all_to_all | solution.py:60
  354.9 1.7 bitcast_reduce_fusion
  356.6 1.4 reshape.208
  358.0 1.1 gather_fusion.1
  359.2 0.2 select_convert_fusion
  359.4 2.3 reshape.211
  361.7 4.1 %multiply_reduce_fusion = f32[64,3584]{1,0:T(8,128)S(1)} fusion(f32[64,2,3584]{2,1,0:T(2,128)} %reshape.211, f32[64,2]{1,0:T(8,128)S(1)} %copy.31), kind=kLoop, calls=%fused_computation.14 | loop fusion | flops 688128 | bytes 2753024 | tf_op jit(solution)/shard_map/reduce_sum | solution.py:67
  365.8 0.9 fusion.20
  (44 shorter events, 2.4 us)
Async XLA Ops:
  87.8 6.5 %copy-start.2 = (bf16[1,1,512,3584]{3,2,1,0:T(8,128)(2,1)S(1)}, bf16[1,1,512,3584]{3,2,1,0:T(8,128)(2,1)}, u32[]{:S(2)}) copy-start(bf16[1,1,512,3584]{3,2,1,0:T(8,128)(2,1)} %param.11) | copy-start | bytes 11010052
  97.9 4.3 %copy-start.1 = (f32[1,2,64,2]{2,3,1,0:T(2,128)S(1)}, f32[1,2,64,2]{2,3,1,0:T(2,128)}, u32[]{:S(2)}) copy-start(f32[1,2,64,2]{2,3,1,0:T(2,128)} %param.13) | copy-start | bytes 3076
  97.9 68.3 %all-to-all-start.1 = ((bf16[16,20,3584]{2,1,0:T(8,128)(2,1)}), bf16[16,20,3584]{2,1,0:T(8,128)(2,1)S(1)}, u32[]{:S(2)}, u32[]{:S(2)}) async-start(bf16[16,20,3584]{2,1,0:T(8,128)(2,1)} %reshape.200), calls=%async_computation.1 | async-start | bytes 5505024 | tf_op jit(solution)/shard_map/all_to_all | solution.py:60
  173.0 4.1 %copy-start = (bf16[1,64,3584]{2,1,0:T(8,128)(2,1)S(1)}, bf16[1,64,3584]{2,1,0:T(8,128)(2,1)}, u32[]{:S(2)}) copy-start(bf16[1,64,3584]{2,1,0:T(8,128)(2,1)} %param.8) | copy-start | bytes 1376260
  177.2 13.7 %collective-permute-start.2 = (bf16[64,3584]{1,0:T(8,128)(2,1)S(1)}, bf16[64,3584]{1,0:T(8,128)(2,1)S(1)}, u32[]{:S(2)}, u32[]{:S(2)}) collective-permute-start(bf16[64,3584]{1,0:T(8,128)(2,1)S(1)} %fusion.13), channel_id=1, source_target_pairs={{32,0},{64,32},{96,64},{128,96},{160,128},{192,160},{224,192},{33,... | collective-permute-start | bytes 1376264 | tf_op jit(solution)/shard_map/ppermute | solution.py:15
  183.0 7.9 %collective-permute-start.1 = (bf16[64,3584]{1,0:T(8,128)(2,1)S(1)}, bf16[64,3584]{1,0:T(8,128)(2,1)S(1)}, u32[]{:S(2)}, u32[]{:S(2)}) collective-permute-start(bf16[64,3584]{1,0:T(8,128)(2,1)S(1)} %fusion.13), channel_id=1, source_target_pairs={{0,1},{2,3},{4,5},{6,7},{8,9},{10,11},{12,13},{14,15},{16,17},{18,... | collective-permute-start | bytes 1376264 | tf_op jit(solution)/shard_map/ppermute | solution.py:15
  184.4 14.1 %collective-permute-start = (bf16[64,3584]{1,0:T(8,128)(2,1)S(1)}, bf16[64,3584]{1,0:T(8,128)(2,1)S(1)}, u32[]{:S(2)}, u32[]{:S(2)}) collective-permute-start(bf16[64,3584]{1,0:T(8,128)(2,1)S(1)} %fusion.13), channel_id=1, source_target_pairs={{0,32},{32,64},{64,96},{96,128},{128,160},{160,192},{192,224},{1,3... | collective-permute-start | bytes 1376264 | tf_op jit(solution)/shard_map/ppermute | solution.py:15
  277.7 6.5 %copy-start.3 = (bf16[1,1,512,3584]{3,2,1,0:T(8,128)(2,1)S(1)}, bf16[1,1,512,3584]{3,2,1,0:T(8,128)(2,1)}, u32[]{:S(2)}) copy-start(bf16[1,1,512,3584]{3,2,1,0:T(8,128)(2,1)} %param.11) | copy-start | bytes 11010052
  287.8 67.1 %all-to-all-start.3 = ((bf16[16,20,3584]{2,1,0:T(8,128)(2,1)}), bf16[16,20,3584]{2,1,0:T(8,128)(2,1)S(1)}, u32[]{:S(2)}, u32[]{:S(2)}) async-start(bf16[16,20,3584]{2,1,0:T(8,128)(2,1)} %reshape.206), calls=%async_computation.3 | async-start | bytes 5505024 | tf_op jit(solution)/shard_map/all_to_all | solution.py:60
where the time goes:
time: 367 us
  blocking collectives  149 us (41%)
  waiting for transfers between devices  138 us (38%)
  local copies, waits for them, and re-layouts  29 us (8%)
  other arithmetic  17.7 us (5%)
  starting transfers between devices  16.8 us (5%)
  matrix products  15.7 us (4%)
    all_to_all x2, blocking collectives, run_section(): lax.all_to_all(outgoing, 'expert', split_axis=0, concat_axis=0, tiled=True)  149 us
    all_to_all x2, waiting for transfers between devices, run_section(): lax.all_to_all(partial_value, 'expert', split_axis=0, concat_axis=0, tile...  127 us
    dot_general x2, matrix products, expert_partial(): both = jnp.dot(flat_rows, weight_in, preferred_element_type=jnp.float32)  12.9 us
    ppermute x3, waiting for transfers between devices, shifted(): return lax.ppermute(block, axis, route)  11.7 us
    ppermute x3, starting transfers between devices, shifted(): return lax.ppermute(block, axis, route)  9.03 us
    reduce_sum x2, other arithmetic, run_section(): jnp.sum(route_weight[:, :, None] * picked.astype(jnp.float32), axis=1)  8.19 us
    all_to_all x2, starting transfers between devices, run_section(): lax.all_to_all(partial_value, 'expert', split_axis=0, concat_axis=0, tile...  7.78 us
  transfers between devices with their start and end apart: 5, of which 4 were waited for; matrix products, arithmetic and copies ran while one was open for 0% of the time, Pallas kernels for 0%

commit v1 on v0

v1 whole, which is shorter than its diff:
```python
import jax
import jax.numpy as jnp
from jax import lax
from jax.experimental import pallas as pl
from jax.experimental.pallas import tpu as pltpu
from jax.sharding import PartitionSpec as P

MESH = pl.DeviceIdType.MESH
BF16, F32 = jnp.bfloat16, jnp.float32

STEPS = 2
EPS = 1e-06
TOK = 64
D = 3584
NG = 4
GC = D // NG
HID = 512
RING = 8
BLK = 80

CHUNKS = ((1, 7), (2, 6), (3, 5), (4, 0))
SEND_ORDER = (1, 7, 2, 6, 3, 5, 4)
PLACE = {k: (j, b) for j, pair in enumerate(CHUNKS) for b, k in enumerate(pair)}


def iota(shape, dim):
    return lax.broadcasted_iota(jnp.int32, shape, dim)


def dot(a, b):
    return jnp.dot(a, b, preferred_element_type=F32)


def dot_rows(a, b):
    return lax.dot_general(a, b, (((0,), (0,)), ((), ())), preferred_element_type=F32)


def kernel(
    states, gain, w_in_hbm, w_out_hbm, routes, route_weights, out,
    w_in, w_out, x_in, x_out, normed, tx, rx, po, pr, zs, ret, lhs, hid, tail,
    z_send, z_recv, f_send, f_recv, p_send, p_recv, r_send, r_recv, s_send, s_recv, w_sem,
):
    pipe = lax.axis_index("pipe")
    expert = lax.axis_index("expert")
    dp = lax.axis_index("dp")
    z, half = expert // 2, expert % 2
    section = dp * 15 + (1 - 2 * dp) * pipe

    def holder(of_section):
        of_dp = of_section // 8
        return (of_dp * 15 + (1 - 2 * of_dp) * of_section, expert, of_dp)

    def on_ring(k):
        return (pipe, (z + k) % RING * 2 + half, dp)

    partner = (pipe, z * 2 + 1 - half, dp)
    after, before = holder((section + 1) % 16), holder((section + 15) % 16)

    barrier = pltpu.get_barrier_semaphore()
    peers = [on_ring(k) for k in range(1, RING)] + [partner, after, before]
    for peer in peers:
        pl.semaphore_signal(barrier, inc=1, device_id=peer, device_id_type=MESH)

    load_in = pltpu.make_async_copy(w_in_hbm.at[0, 0], w_in, w_sem.at[0])
    load_out = pltpu.make_async_copy(w_out_hbm.at[0, 0], w_out, w_sem.at[1])
    load_in.start()
    load_out.start()

    def send(src, dst, sems, index, peer):
        copy = pltpu.make_async_remote_copy(
            src_ref=src, dst_ref=dst, send_sem=sems[0].at[index], recv_sem=sems[1].at[index],
            device_id=peer, device_id_type=MESH,
        )
        copy.start()
        return copy

    ra, ca = iota((16, 64), 0), iota((16, 64), 1)
    same = (ra // 4 == ca // 16) & (ra % 4 == ca % 4)
    unstack = [jnp.where(same & (ca % 16 // 4 == g), 1.0, 0.0).astype(BF16) for g in range(NG)]
    rb, cb = iota((64, 64), 0), iota((64, 64), 1)
    restack = jnp.where(
        (rb // 16 == cb % 16 // 4) & (rb % 16 // 4 == cb // 16) & (rb % 4 == cb % 4), 1.0, 0.0
    ).astype(BF16)
    below = jnp.where(iota((TOK, TOK), 0) > iota((TOK, TOK), 1), 1.0, 0.0).astype(BF16)
    col = iota((TOK, 128), 1)
    expert_of = (z + col // 16) % RING

    def routing(step):
        first = routes[0, step, :, 0:1] == expert_of
        second = routes[0, step, :, 1:2] == expert_of
        named = jnp.where(first | second, 1.0, 0.0)
        weight = jnp.where(first, route_weights[0, step, :, 0:1], 0.0) + jnp.where(
            second, route_weights[0, step, :, 1:2], 0.0
        )
        slot = dot(below, named.astype(BF16)).astype(jnp.int32)
        in_main = slot == col % 16
        in_tail = slot == 16 + col % 4
        masks = [in_main] + [in_tail & (col % 16 // 4 == g) for g in range(NG)]
        pick = [jnp.where(m, named, 0.0).astype(BF16) for m in masks]
        mix = [jnp.where(m, weight, 0.0) for m in masks]
        high = [m.astype(BF16) for m in mix]
        low = [(m - h.astype(F32)).astype(BF16) for m, h in zip(mix, high)]

        def whole(parts):
            return [jnp.concatenate([parts[0], parts[1 + g]], axis=1) for g in range(NG)]

        return whole(pick), whole(high), whole(low)

    waits = []
    shift = []
    for step in range(STEPS):
        pick, high, low = routing(step)

        if step == 0:
            for g in range(NG):
                x_in[step, g] = states[0, :, g * GC : (g + 1) * GC]
        else:
            for copy in shift:
                copy.wait_recv()
            for g in range(NG):
                x_in[step, g] = jnp.where(section == 0, jnp.zeros((), BF16), x_in[step, g])
        squares = jnp.zeros((TOK, 1), F32)
        for g in range(NG):
            x = x_in[step, g].astype(F32)
            squares = squares + jnp.sum(x * x, axis=1, keepdims=True)
        scale = lax.rsqrt(squares / D + EPS)
        rest = jnp.zeros((128, GC), F32)
        for g in range(NG):
            x = x_in[step, g].astype(F32)
            normed = (x * scale * gain[0:1, g * GC : (g + 1) * GC]).astype(BF16)
            rows = dot_rows(pick[g], normed)
            tx[step, :, g * 16 : (g + 1) * 16, :] = rows[:128].astype(BF16).reshape(RING, 16, GC)
            rest = rest + rows[128:]
        tx[step, :, 64:80, :] = rest.astype(BF16).reshape(RING, 16, GC)

        if step == 0:
            pl.semaphore_wait(barrier, len(peers))

        j0, b0 = PLACE[0]
        forward = {}
        forward[0] = send(
            tx.at[step, 0], rx.at[step, j0, 2 + b0], (f_send.at[step], f_recv.at[step]), 0, partner
        )
        arrive = {}
        for k in SEND_ORDER:
            j, b = PLACE[k]
            arrive[k] = send(
                tx.at[step, k], rx.at[step, j, b], (z_send.at[step], z_recv.at[step]), k, on_ring(k)
            )
        rx[step, j0, b0] = tx[step, 0]

        def pass_on(j):
            for b, k in enumerate(CHUNKS[j]):
                if k:
                    arrive[k].wait_recv()
                    forward[k] = send(
                        rx.at[step, j, b], rx.at[step, j, 2 + b],
                        (f_send.at[step], f_recv.at[step]), k, partner,
                    )

        partial = {}

        def compute(j):
            for k in CHUNKS[j]:
                forward[k].wait_recv()
            for g in range(NG):
                columns = slice(g * GC, (g + 1) * GC)
                lhs[0:64, columns] = rx[step, j, :, g * 16 : (g + 1) * 16, :].reshape(64, GC)
                tails = rx[step, j, :, 64:80, :].reshape(64, GC)
                lhs[64:80, columns] = dot(unstack[g], tails).astype(BF16)

            if step == 0 and j == 0:
                load_in.wait()

            @pl.loop(0, 2)
            def _(n):
                at = pl.multiple_of(n * 256, 256)
                gate = dot(lhs[...], w_in[:, pl.ds(at, 256)])
                up = dot(lhs[...], w_in[:, pl.ds(pl.multiple_of(at + HID, 256), 256)])
                hid[:, pl.ds(at, 256)] = (gate / (1.0 + jnp.exp(-gate)) * up).astype(BF16)

            if step == 0 and j == 0:
                load_out.wait()

            @pl.loop(0, NG)
            def _(g):
                at = pl.multiple_of(g * GC, 128)
                y = dot(hid[...], w_out[:, pl.ds(at, GC)]).astype(BF16)
                row = pl.multiple_of(g * 16, 16)
                po[step, j, :, pl.ds(row, 16), :] = y[:64].reshape(4, 16, GC)
                tail[pl.ds(row, 16), :] = y[64:]

            po[step, j, :, 64:80, :] = dot(restack, tail[...]).astype(BF16).reshape(4, 16, GC)
            for b, k in enumerate(CHUNKS[j]):
                partial[k] = send(
                    po.at[step, j, 2 + b], pr.at[step, j, b],
                    (p_send.at[step], p_recv.at[step]), k, partner,
                )

        back = {}

        def give_back(j):
            for b, k in enumerate(CHUNKS[j]):
                partial[k].wait_recv()
                total = po[step, j, b].astype(F32) + pr[step, j, b].astype(F32)
                if k == 0:
                    ret[step, 0] = total.astype(BF16)
                else:
                    zs[step, j, b] = total.astype(BF16)
                    back[k] = send(
                        zs.at[step, j, b], ret.at[step, k],
                        (r_send.at[step], r_recv.at[step]), k, on_ring(RING - k),
                    )

        for tick in range(len(CHUNKS) + 2):
            if tick < len(CHUNKS):
                pass_on(tick)
            if 1 <= tick <= len(CHUNKS):
                compute(tick - 1)
            if tick >= 2:
                give_back(tick - 2)

        for k in back:
            back[k].wait_recv()
        for g in range(NG):
            main = ret[step, :, g * 16 : (g + 1) * 16, :].reshape(128, GC)
            tails = ret[step, :, 64:80, :].reshape(128, GC)
            rows = jnp.concatenate([main, tails], axis=0)
            total = dot(high[g], rows) + dot(low[g], rows)
            y = (x_in[step, g].astype(F32) + total).astype(BF16)
            if step + 1 < STEPS:
                x_out[g] = y
                shift.append(send(x_out.at[g], x_in.at[step + 1, g], (s_send, s_recv), g, after))
            else:
                out[0, :, g * GC : (g + 1) * GC] = y
        for copies in (arrive, forward, partial, back):
            waits.extend(copies.values())

    for copy in waits + shift:
        copy.wait_send()


def body(states, norm_gain, w_in, w_out, routes, route_weights):
    vmem, hbm = pl.BlockSpec(memory_space=pltpu.VMEM), pl.BlockSpec(memory_space=pl.ANY)
    sems = pltpu.SemaphoreType.DMA
    n = len(CHUNKS)
    return pl.pallas_call(
        kernel,
        out_shape=jax.ShapeDtypeStruct(states.shape, BF16),
        in_specs=[vmem, vmem, hbm, hbm, vmem, vmem],
        out_specs=vmem,
        scratch_shapes=[
            pltpu.VMEM((D, 2 * HID), BF16),
            pltpu.VMEM((HID, D), BF16),
            pltpu.VMEM((STEPS, NG, TOK, GC), BF16),
            pltpu.VMEM((NG, TOK, GC), BF16),
            pltpu.VMEM((NG, TOK, GC), BF16),
            pltpu.VMEM((STEPS, RING, BLK, GC), BF16),
            pltpu.VMEM((STEPS, n, 4, BLK, GC), BF16),
            pltpu.VMEM((STEPS, n, 4, BLK, GC), BF16),
            pltpu.VMEM((STEPS, n, 2, BLK, GC), BF16),
            pltpu.VMEM((STEPS, n, 2, BLK, GC), BF16),
            pltpu.VMEM((STEPS, RING, BLK, GC), BF16),
            pltpu.VMEM((BLK, D), BF16),
            pltpu.VMEM((BLK, HID), BF16),
            pltpu.VMEM((64, GC), BF16),
        ]
        + [sems((STEPS, RING))] * 8
        + [sems((NG,))] * 2
        + [sems((2,))],
        compiler_params=pltpu.CompilerParams(
            collective_id=0, has_side_effects=True, vmem_limit_bytes=56 * 2**20
        ),
        cost_estimate=pl.CostEstimate(
            flops=2 * 2 * 320 * 5505024, bytes_accessed=12 * 2**20, transcendentals=0
        ),
        name="cascade",
    )(states, norm_gain, w_in, w_out, routes, route_weights)


def solution(mesh):
    in_specs = (
        P(("pipe", "dp"), "expert", None),
        P(("pipe", "dp"), None),
        P(("pipe", "dp"), "expert", None, None),
        P(("pipe", "dp"), "expert", None, None),
        P(("pipe", "dp"), None, "expert", None),
        P(("pipe", "dp"), None, "expert", None),
    )
    out_specs = P(("pipe", "dp"), "expert", None)
    return jax.shard_map(body, mesh=mesh, in_specs=in_specs, out_specs=out_specs, check_vma=False)
```

time: 367 us -> 155 us (0.42)
  the two profiles are of different devices: /device:TPU:2 before, /device:TPU:8 now
where the time goes in v1:
time: 155 us
  Pallas kernels  150 us (97%)
  local copies, waits for them, and re-layouts  4.63 us (3%)
    pallas_call x1, Pallas kernels, body(): pl.pallas_call(kernel, out_shape=jax.ShapeDtypeStruct(states.shape, BF16)...  150 us
    unnamed x3, local copies, waits for them, and re-layouts  4.63 us

profile of v1, /device:TPU:8, one launch (start us, length us, event | category | flops | bytes accessed | tf_op | source)
XLA Modules:
  0.0 155.0 jit_solution(9915178173216684098)
XLA Ops:
  0.0 1.4 copy.7.routes
  1.4 1.4 copy.8.route_weights
  2.8 150.3 %cascade.1 = bf16[1,64,3584]{2,1,0:T(8,128)(2,1)} custom-call(bf16[1,64,3584]{2,1,0:T(8,128)(2,1)} %states.1, f32[1,3584]{1,0:T(1,128)} %gain.1, bf16[1,1,3584,1024]{3,2,1,0:T(8,128)(2,1)} %w_in_hbm.1, bf16[1,1,512,3584]{3,2,1,0:T(8,128)(2,1)} %w_out_hbm.1, s32[1,2,64,2]{3,2,1,0:T(8,128)} %copy.7.routes, f32[1,2,64,2]{3,2,1,0:T(8,128)} %copy.8.route_weights), custom_call_target="tpu_custom_call" | custom-call | flops 7046430720 | bytes 12582912 | tf_op jit(solution)/shard_map/cascade/pallas_call | solution.py:247
  153.2 1.8 %copy.10 = bf16[1,64,3584]{2,1,0:T(8,128)(2,1)} copy(bf16[1,64,3584]{2,1,0:T(8,128)(2,1)} %cascade.1) | data formatting | bytes 917504

commit v2 on v1

--- a/solution.py
+++ b/solution.py
@@ -18,9 +18,13 @@
 RING = 8
 BLK = 80
 
-CHUNKS = ((1, 7), (2, 6), (3, 5), (4, 0))
-SEND_ORDER = (1, 7, 2, 6, 3, 5, 4)
-PLACE = {k: (j, b) for j, pair in enumerate(CHUNKS) for b, k in enumerate(pair)}
+CHUNKS = ((1, 0), (4, 7), (2, 6), (5, 3))
+SEND_ORDER = (7, 5, 3, 2, 6, 1, 4)
+AHEAD = 3
+PROGRAM = (
+    ("F", 7), ("F", 3), ("F", 5), ("F", 2), ("F", 6), ("C", 3), ("F", 4), ("C", 2),
+    ("G", 3), ("F", 1), ("C", 1), ("G", 2), ("C", 0), ("G", 1), ("G", 0),
+)
 
 
 def iota(shape, dim):
@@ -37,13 +41,15 @@
 
 def kernel(
     states, gain, w_in_hbm, w_out_hbm, routes, route_weights, out,
-    w_in, w_out, x_in, x_out, normed, tx, rx, po, pr, zs, ret, lhs, hid, tail,
+    w_in, w_out, x_in, x_out, pick, high, low, tx, rx, po, pr, zs, ret, lhs, hid, tail,
     z_send, z_recv, f_send, f_recv, p_send, p_recv, r_send, r_recv, s_send, s_recv, w_sem,
 ):
     pipe = lax.axis_index("pipe")
     expert = lax.axis_index("expert")
     dp = lax.axis_index("dp")
     z, half = expert // 2, expert % 2
+    first_chunk = [which for act, which in PROGRAM if act == "C"][0]
+    PLACE = {k: (j, b) for j, pair in enumerate(CHUNKS) for b, k in enumerate(pair)}
     section = dp * 15 + (1 - 2 * dp) * pipe
 
     def holder(of_section):
@@ -85,40 +91,54 @@
     col = iota((TOK, 128), 1)
     expert_of = (z + col // 16) % RING
 
-    def routing(step):
-        first = routes[0, step, :, 0:1] == expert_of
-        second = routes[0, step, :, 1:2] == expert_of
+    def routing(step, stage):
+        ids = jnp.transpose(routes[0, step].astype(F32)).astype(jnp.int32)
+        first, second = ids[:, 0:1] == expert_of, ids[:, 1:2] == expert_of
         named = jnp.where(first | second, 1.0, 0.0)
-        weight = jnp.where(first, route_weights[0, step, :, 0:1], 0.0) + jnp.where(
-            second, route_weights[0, step, :, 1:2], 0.0
+        slot = dot(below, named.astype(BF16)).astype(jnp.int32)
+        in_main, in_tail = slot == col % 16, slot == 16 + col % 4
+        if stage == "pick":
+            value = named
+        else:
+            weights = jnp.transpose(route_weights[0, step])
+            value = jnp.where(first, weights[:, 0:1], 0.0) + jnp.where(second, weights[:, 1:2], 0.0)
+        for part in range(1 + NG):
+            mask = in_main if part == 0 else in_tail & (col % 16 // 4 == part - 1)
+            entry = jnp.where(mask, value, 0.0)
+            near = entry.astype(BF16)
+            rest = (entry - near.astype(F32)).astype(BF16)
+            for g in range(NG) if part == 0 else (part - 1,):
+                half = slice(0, 128) if part == 0 else slice(128, 256)
+                if stage == "pick":
+                    pick[step, g, :, half] = near
+                else:
+                    high[step, g, :, half] = near
+                    low[step, g, :, half] = rest
+
+    def hand_on(g):
+        return pltpu.make_async_remote_copy(
+            src_ref=x_out.at[g], dst_ref=x_in.at[1, g], send_sem=s_send.at[g], recv_sem=s_recv.at[g],
+            device_id=after, device_id_type=MESH,
         )
-        slot = dot(below, named.astype(BF16)).astype(jnp.int32)
-        in_main = slot == col % 16
-        in_tail = slot == 16 + col % 4
-        masks = [in_main] + [in_tail & (col % 16 // 4 == g) for g in range(NG)]
-        pick = [jnp.where(m, named, 0.0).astype(BF16) for m in masks]
-        mix = [jnp.where(m, weight, 0.0) for m in masks]
-        high = [m.astype(BF16) for m in mix]
-        low = [(m - h.astype(F32)).astype(BF16) for m, h in zip(mix, high)]
-
-        def whole(parts):
-            return [jnp.concatenate([parts[0], parts[1 + g]], axis=1) for g in range(NG)]
-
-        return whole(pick), whole(high), whole(low)
 
     waits = []
-    shift = []
     for step in range(STEPS):
-        pick, high, low = routing(step)
+        if step == 0:
+            routing(step, "pick")
 
         if step == 0:
             for g in range(NG):
                 x_in[step, g] = states[0, :, g * GC : (g + 1) * GC]
         else:
-            for copy in shift:
-                copy.wait_recv()
-            for g in range(NG):
-                x_in[step, g] = jnp.where(section == 0, jnp.zeros((), BF16), x_in[step, g])
+            @pl.when(section == 0)
+            def _():
+                x_in[step] = jnp.zeros((NG, TOK, GC), BF16)
+
+            @pl.when(section > 0)
+            def _():
+                for g in range(NG):
+                    hand_on(g).wait_recv()
+
         squares = jnp.zeros((TOK, 1), F32)
         for g in range(NG):
             x = x_in[step, g].astype(F32)
@@ -128,7 +148,7 @@
         for g in range(NG):
             x = x_in[step, g].astype(F32)
             normed = (x * scale * gain[0:1, g * GC : (g + 1) * GC]).astype(BF16)
-            rows = dot_rows(pick[g], normed)
+            rows = dot_rows(pick[step, g], normed)
             tx[step, :, g * 16 : (g + 1) * 16, :] = rows[:128].astype(BF16).reshape(RING, 16, GC)
             rest = rest + rows[128:]
         tx[step, :, 64:80, :] = rest.astype(BF16).reshape(RING, 16, GC)
@@ -142,21 +162,31 @@
             tx.at[step, 0], rx.at[step, j0, 2 + b0], (f_send.at[step], f_recv.at[step]), 0, partner
         )
         arrive = {}
-        for k in SEND_ORDER:
+
+        def dispatch(k):
             j, b = PLACE[k]
             arrive[k] = send(
                 tx.at[step, k], rx.at[step, j, b], (z_send.at[step], z_recv.at[step]), k, on_ring(k)
             )
+
+        todo = list(SEND_ORDER)
+        for _ in range(AHEAD):
+            dispatch(todo.pop(0))
         rx[step, j0, b0] = tx[step, 0]
-
-        def pass_on(j):
-            for b, k in enumerate(CHUNKS[j]):
-                if k:
-                    arrive[k].wait_recv()
-                    forward[k] = send(
-                        rx.at[step, j, b], rx.at[step, j, 2 + b],
-                        (f_send.at[step], f_recv.at[step]), k, partner,
-                    )
+        if step == 0:
+            for later in range(STEPS):
+                if later:
+                    routing(later, "pick")
+                routing(later, "mix")
+
+        def pass_on(k):
+            arrive[k].wait_recv()
+            if todo:
+                dispatch(todo.pop(0))
+            j, b = PLACE[k]
+            forward[k] = send(
+                rx.at[step, j, b], rx.at[step, j, 2 + b], (f_send.at[step], f_recv.at[step]), k, partner
+            )
 
         partial = {}
 
@@ -169,7 +199,7 @@
                 tails = rx[step, j, :, 64:80, :].reshape(64, GC)
                 lhs[64:80, columns] = dot(unstack[g], tails).astype(BF16)
 
-            if step == 0 and j == 0:
+            if step == 0 and j == first_chunk:
                 load_in.wait()
 
             @pl.loop(0, 2)
@@ -179,7 +209,7 @@
                 up = dot(lhs[...], w_in[:, pl.ds(pl.multiple_of(at + HID, 256), 256)])
                 hid[:, pl.ds(at, 256)] = (gate / (1.0 + jnp.exp(-gate)) * up).astype(BF16)
 
-            if step == 0 and j == 0:
+            if step == 0 and j == first_chunk:
                 load_out.wait()
 
             @pl.loop(0, NG)
@@ -212,13 +242,8 @@
                         (r_send.at[step], r_recv.at[step]), k, on_ring(RING - k),
                     )
 
-        for tick in range(len(CHUNKS) + 2):
-            if tick < len(CHUNKS):
-                pass_on(tick)
-            if 1 <= tick <= len(CHUNKS):
-                compute(tick - 1)
-            if tick >= 2:
-                give_back(tick - 2)
+        for act, which in PROGRAM:
+            {"F": pass_on, "C": compute, "G": give_back}[act](which)
 
         for k in back:
             back[k].wait_recv()
@@ -226,18 +251,27 @@
             main = ret[step, :, g * 16 : (g + 1) * 16, :].reshape(128, GC)
             tails = ret[step, :, 64:80, :].reshape(128, GC)
             rows = jnp.concatenate([main, tails], axis=0)
-            total = dot(high[g], rows) + dot(low[g], rows)
+            total = dot(high[step, g], rows) + dot(low[step, g], rows)
             y = (x_in[step, g].astype(F32) + total).astype(BF16)
             if step + 1 < STEPS:
                 x_out[g] = y
-                shift.append(send(x_out.at[g], x_in.at[step + 1, g], (s_send, s_recv), g, after))
+
+                @pl.when(section < 15)
+                def _():
+                    hand_on(g).start()
+
             else:
                 out[0, :, g * GC : (g + 1) * GC] = y
         for copies in (arrive, forward, partial, back):
             waits.extend(copies.values())
 
-    for copy in waits + shift:
+    for copy in waits:
         copy.wait_send()
+
+    @pl.when(section < 15)
+    def _():
+        for g in range(NG):
+            hand_on(g).wait_send()
 
 
 def body(states, norm_gain, w_in, w_out, routes, route_weights):
@@ -254,7 +288,9 @@
             pltpu.VMEM((HID, D), BF16),
             pltpu.VMEM((STEPS, NG, TOK, GC), BF16),
             pltpu.VMEM((NG, TOK, GC), BF16),
-            pltpu.VMEM((NG, TOK, GC), BF16),
+            pltpu.VMEM((STEPS, NG, TOK, 256), BF16),
+            pltpu.VMEM((STEPS, NG, TOK, 256), BF16),
+            pltpu.VMEM((STEPS, NG, TOK, 256), BF16),
             pltpu.VMEM((STEPS, RING, BLK, GC), BF16),
             pltpu.VMEM((STEPS, n, 4, BLK, GC), BF16),
             pltpu.VMEM((STEPS, n, 4, BLK, GC), BF16),
@@ -275,7 +311,7 @@
             flops=2 * 2 * 320 * 5505024, bytes_accessed=12 * 2**20, transcendentals=0
         ),
         name="cascade",
-    )(states, norm_gain, w_in, w_out, routes, route_weights)
+    )(states, norm_gain, w_in, w_out, jnp.swapaxes(routes, 2, 3), jnp.swapaxes(route_weights, 2, 3))
 
 
 def solution(mesh):

time: 155 us -> 144 us (0.929)
  the two profiles are of different devices: /device:TPU:8 before, /device:TPU:2 now
where the time goes in v2:
time: 144 us; the launch traced here: 142 us
  Pallas kernels  140 us (97%)
  local copies, waits for them, and re-layouts  1.82 us (1%)
    pallas_call x1, Pallas kernels, body(): pl.pallas_call(kernel, out_shape=jax.ShapeDtypeStruct(states.shape, BF16)...  140 us

profile of v2, /device:TPU:2, one launch (start us, length us, event | category | flops | bytes accessed | tf_op | source)
XLA Modules:
  0.0 141.8 jit_solution(9456137975625704122)
XLA Ops:
  0.0 140.0 %cascade.1 = bf16[1,64,3584]{2,1,0:T(8,128)(2,1)} custom-call(bf16[1,64,3584]{2,1,0:T(8,128)(2,1)} %states.1, f32[1,3584]{1,0:T(1,128)} %gain.1, bf16[1,1,3584,1024]{3,2,1,0:T(8,128)(2,1)} %w_in_hbm.1, bf16[1,1,512,3584]{3,2,1,0:T(8,128)(2,1)} %w_out_hbm.1, s32[1,2,2,64]{3,2,1,0:T(2,128)} %bitcast.2, f32[1,2,2,64]{3,2,1,0:T(2,128)} %bitcast.3), custom_call_target="tpu_custom_call" | custom-call | flops 7046430720 | bytes 12582912 | tf_op jit(solution)/shard_map/cascade/pallas_call | solution.py:281
  140.0 1.8 %copy.8 = bf16[1,64,3584]{2,1,0:T(8,128)(2,1)} copy(bf16[1,64,3584]{2,1,0:T(8,128)(2,1)} %cascade.1) | data formatting | bytes 917504

commit v3 on v2

--- a/solution.py
+++ b/solution.py
@@ -42,7 +42,7 @@
 def kernel(
     states, gain, w_in_hbm, w_out_hbm, routes, route_weights, out,
     w_in, w_out, x_in, x_out, pick, high, low, tx, rx, po, pr, zs, ret, lhs, hid, tail,
-    z_send, z_recv, f_send, f_recv, p_send, p_recv, r_send, r_recv, s_send, s_recv, w_sem,
+    z_send, z_recv, f_send, f_recv, p_send, p_recv, r_send, r_recv, s_send, s_recv, w_sem, x_sem,
 ):
     pipe = lax.axis_index("pipe")
     expert = lax.axis_index("expert")
@@ -61,6 +61,13 @@
 
     partner = (pipe, z * 2 + 1 - half, dp)
     after, before = holder((section + 1) % 16), holder((section + 15) % 16)
+
+    loads = [
+        pltpu.make_async_copy(states.at[0, :, pl.ds(g * GC, GC)], x_in.at[0, g], x_sem.at[g])
+        for g in range(NG)
+    ]
+    for load in loads:
+        load.start()
 
     barrier = pltpu.get_barrier_semaphore()
     peers = [on_ring(k) for k in range(1, RING)] + [partner, after, before]
@@ -127,8 +134,8 @@
             routing(step, "pick")
 
         if step == 0:
-            for g in range(NG):
-                x_in[step, g] = states[0, :, g * GC : (g + 1) * GC]
+            for load in loads:
+                load.wait()
         else:
             @pl.when(section == 0)
             def _():
@@ -281,7 +288,7 @@
     return pl.pallas_call(
         kernel,
         out_shape=jax.ShapeDtypeStruct(states.shape, BF16),
-        in_specs=[vmem, vmem, hbm, hbm, vmem, vmem],
+        in_specs=[hbm, vmem, hbm, hbm, vmem, vmem],
         out_specs=vmem,
         scratch_shapes=[
             pltpu.VMEM((D, 2 * HID), BF16),
@@ -303,7 +310,7 @@
         ]
         + [sems((STEPS, RING))] * 8
         + [sems((NG,))] * 2
-        + [sems((2,))],
+        + [sems((2,)), sems((NG,))],
         compiler_params=pltpu.CompilerParams(
             collective_id=0, has_side_effects=True, vmem_limit_bytes=56 * 2**20
         ),

time: 144 us -> 147 us (1.021)
  Pallas kernels: 140 us -> 142 us
    pallas_call x1, Pallas kernels: 140 us -> 142 us  [body(): pl.pallas_call(kernel, out_shape=jax.ShapeDtypeStruct(states.shape, BF16)...]
where the time goes in v3:
time: 147 us; the launch traced here: 144 us
  Pallas kernels  142 us (97%)
  local copies, waits for them, and re-layouts  1.82 us (1%)
    pallas_call x1, Pallas kernels, body(): pl.pallas_call(kernel, out_shape=jax.ShapeDtypeStruct(states.shape, BF16)...  142 us

profile of v3, /device:TPU:2, one launch (start us, length us, event | category | flops | bytes accessed | tf_op | source)
XLA Modules:
  0.0 143.9 jit_solution(5667266822486738193)
XLA Ops:
  0.0 142.1 %cascade.1 = bf16[1,64,3584]{2,1,0:T(8,128)(2,1)} custom-call(bf16[1,64,3584]{2,1,0:T(8,128)(2,1)} %states.1, f32[1,3584]{1,0:T(1,128)} %gain.1, bf16[1,1,3584,1024]{3,2,1,0:T(8,128)(2,1)} %w_in_hbm.1, bf16[1,1,512,3584]{3,2,1,0:T(8,128)(2,1)} %w_out_hbm.1, s32[1,2,2,64]{3,2,1,0:T(2,128)} %bitcast.2, f32[1,2,2,64]{3,2,1,0:T(2,128)} %bitcast.3), custom_call_target="tpu_custom_call" | custom-call | flops 7046430720 | bytes 12582912 | tf_op jit(solution)/shard_map/cascade/pallas_call | solution.py:288
  142.1 1.8 %copy.8 = bf16[1,64,3584]{2,1,0:T(8,128)(2,1)} copy(bf16[1,64,3584]{2,1,0:T(8,128)(2,1)} %cascade.1) | data formatting | bytes 917504
